TPU v7x, 512 devices: a whole 4x8x8 slice. The times are simulated.
512 devices in a mesh: row: 16 (over x_hi, y), col: 32 (over z, x_lo, core).
Axes of the slice: x: 4 (x_hi: 2, x_lo: 2; x = x_hi * 2 + x_lo), y: 8, z: 8, core: 2. Of those that a mesh axis runs over, the one named last changes fastest.
Arguments:
- tiles: bfloat16 [1024, 1024, 1024], P(('row', 'col')), may hold values from 0 to 12288, as said below
- tile_blocks: int32 [1024, 2], P(('row', 'col')), may hold values from 0 to 63, as said below
- tile_count: int32 [512], P(('row', 'col')), may hold values from 1 to 2, as said below
- factor: float32 [2, 2, 16, 32, 32, 128], P(None, None, 'row', 'col'), may hold values from 0.2 to 5
Outputs:
- factor_out: float32 [2, 2, 16, 32, 32, 128], P(None, None, 'row', 'col')
Inputs may be any that keep to these rules, and one draw needn't show every extreme that they name: `tile_blocks`: slot s belongs to the device of index s // 2 along row+col, with grid indices (r, c); its (i, j) has i <= j, i % 16 == r and j % 32 == c. A device's live slots are its first tile_count entries. `tiles`: tiles are nonnegative.
All inputs are finite; a program needn't handle non-finite values.
Results may differ from a plain program's by a relative error of at most 0.0003.
Values may be sent and summed in bfloat16 or wider, within the bound.
A program may use at most 64 MiB of HBM per device.

v0:
```python
import jax
import jax.numpy as jnp
from jax import lax
from jax.sharding import PartitionSpec as P

ITERS = 2


def self_gram(flattened):
    return lax.dot_general(
        flattened, flattened, (((0,), (0,)), ((), ())), preferred_element_type=jnp.float32
    )


def shards(tiles, tile_blocks, tile_count, factor):
    row_count = lax.axis_size("row")
    column_count = lax.axis_size("col")
    column_blocks, multiple, _, _, slice_rows, rank_width = factor.shape
    block_rows = slice_rows * column_count
    held = factor
    for sweep in range(ITERS):
        halves = held.astype(jnp.bfloat16)
        gathered = lax.all_gather(halves, "col", axis=3, tiled=True)
        row_panel = gathered.reshape(column_blocks * multiple, block_rows, rank_width)
        gram_matrix = lax.psum(self_gram(halves.reshape(-1, rank_width)), ("row", "col"))
        spread = lax.all_gather(halves, "row", axis=2, tiled=True)
        spread = spread.reshape(column_blocks, multiple * row_count, 1, slice_rows, rank_width)
        arrived = lax.all_to_all(spread, "col", split_axis=1, concat_axis=2, tiled=True)
        column_panel = arrived.reshape(column_blocks, block_rows, rank_width)

        def add_tile(slot_index, totals_pair):
            row_total, column_total = totals_pair
            block_tile = lax.dynamic_index_in_dim(tiles, slot_index, 0, keepdims=False)
            position = lax.dynamic_index_in_dim(tile_blocks, slot_index, 0, keepdims=False)
            row_block = position[0]
            column_block = position[1]
            row_slot = row_block // row_count
            column_slot = column_block // column_count
            right_rows = lax.dynamic_index_in_dim(column_panel, column_slot, 0, keepdims=False)
            left_rows = lax.dynamic_index_in_dim(row_panel, row_slot, 0, keepdims=False)
            row_term = jnp.dot(block_tile, right_rows, preferred_element_type=jnp.float32)
            column_term = lax.dot_general(
                block_tile, left_rows, (((0,), (0,)), ((), ())), preferred_element_type=jnp.float32
            )
            weight = (row_block != column_block).astype(jnp.float32)
            row_old = lax.dynamic_index_in_dim(row_total, row_slot, 0, keepdims=False)
            row_total = lax.dynamic_update_index_in_dim(row_total, row_old + row_term, row_slot, 0)
            column_old = lax.dynamic_index_in_dim(column_total, column_slot, 0, keepdims=False)
            column_total = lax.dynamic_update_index_in_dim(
                column_total, column_old + weight * column_term, column_slot, 0
            )
            return (row_total, column_total)

        row_start = jnp.zeros((column_blocks * multiple, block_rows, rank_width), jnp.float32)
        column_start = jnp.zeros((column_blocks, block_rows, rank_width), jnp.float32)
        row_total, column_total = lax.fori_loop(
            0, tile_count[0], add_tile, (row_start, column_start)
        )
        row_pieces = row_total.reshape(
            column_blocks, multiple, column_count, slice_rows, rank_width
        )
        summed = lax.psum_scatter(row_pieces, "col", scatter_dimension=2, tiled=True)
        product = summed.reshape(column_blocks, multiple, slice_rows, rank_width)
        pieces = column_total.reshape(column_blocks, column_count, slice_rows, rank_width)
        moved_pieces = lax.all_to_all(pieces, "col", split_axis=1, concat_axis=1, tiled=True)
        moved_pieces = moved_pieces.reshape(
            column_blocks, multiple, row_count, slice_rows, rank_width
        )
        returned = lax.all_to_all(moved_pieces, "row", split_axis=2, concat_axis=2, tiled=True)
        product = product + jnp.sum(returned, axis=2)
        current = held.reshape(column_blocks, multiple, slice_rows, rank_width)
        denominator = jnp.dot(
            current.reshape(-1, rank_width), gram_matrix, precision=lax.Precision.HIGHEST
        ).reshape(current.shape)
        current = current * (0.5 + 0.5 * product / denominator)
        held = current.reshape(factor.shape)
    return held


def solution(mesh):
    in_specs = (
        P(("row", "col"), None, None),
        P(("row", "col"), None),
        P(("row", "col")),
        P(None, None, "row", "col", None, None),
    )
    out_specs = P(None, None, "row", "col", None, None)
    return jax.shard_map(shards, mesh=mesh, in_specs=in_specs, out_specs=out_specs, check_vma=False)
```

profile of v0, /device:TPU:1, one launch (start us, length us, event | category | flops | bytes accessed | tf_op | source)
XLA Modules:
  0.0 655.7 jit_solution(4983007763306921730)
XLA Ops:
  7.4 1.5 convert_element_type.22
  8.8 38.1 %all_gather.12 = bf16[2,2,16,1,32,128]{5,4,3,2,1,0:T(8,128)(2,1)S(1)} all-gather(bf16[2,2,1,1,32,128]{5,4,3,2,1,0:T(8,128)(2,1)} %convert_element_type.22), channel_id=1, replica_groups=mesh['row'=16,'col'=32] {'row'}, dimensions={2}, use_global_device_ids=true | all-gather | bytes 557056 | tf_op jit(solution)/shard_map/all_gather | solution.py:26
  46.9 0.9 copy.25
  47.8 18.5 %all-to-all-start = ((bf16[2,32,1,32,128]{4,3,0,2,1:T(8,128)(2,1)}), bf16[2,32,1,32,128]{4,3,0,2,1:T(8,128)(2,1)S(1)}, u32[]{:S(2)}, u32[]{:S(2)}) async-start(bf16[2,32,1,32,128]{4,3,0,2,1:T(8,128)(2,1)} %bitcast.20), calls=%async_computation | async-start | bytes 1048576 | tf_op jit(solution)/shard_map/all_to_all | solution.py:28
  66.4 0.8 convolution_bitcast_fusion.1
  67.3 17.2 %all-to-all-done = bf16[2,32,1,32,128]{4,3,0,2,1:T(8,128)(2,1)S(1)} async-done(((bf16[2,32,1,32,128]{4,3,0,2,1:T(8,128)(2,1)}), bf16[2,32,1,32,128]{4,3,0,2,1:T(8,128)(2,1)S(1)}, u32[]{:S(2)}, u32[]{:S(2)}) %all-to-all-start) | async-done | bytes 524320 | tf_op jit(solution)/shard_map/all_to_all | solution.py:28
  84.5 0.9 copy.26
  85.4 0.1 broadcast.33.clone
  85.6 28.6 %while.30 = (s32[]{:T(128)}, f32[4,1024,128]{2,1,0:T(8,128)S(1)}, f32[2,1024,128]{2,1,0:T(8,128)S(1)}, s32[]{:T(128)}, s32[2,2]{1,0:T(2,128)S(1)}, /*index=5*/bf...) while((s32[]{:T(128)}, f32[4,1024,128]{2,1,0:T(8,128)S(1)}, ...), condition=%wide.region_1.2_spmd, body=%wide.region_0.0_spmd.sunk | while | flops 537264128 | bytes 11010713 | solution.py:56
  86.3 0.6 fusion.109
  92.2 0.9 constant_dynamic-slice_fusion.11
  93.1 0.3 copy-done.1
  93.4 2.3 fusion.110
  97.0 2.5 fusion.111
  100.3 0.6 fusion.109
  106.2 0.9 constant_dynamic-slice_fusion.11
  107.1 0.3 copy-done.1
  107.4 2.3 fusion.110
  111.0 2.5 fusion.111
  114.2 1.6 copy.27
  115.9 32.9 %all_to_all.38 = f32[2,32,32,128]{3,2,0,1:T(8,128)S(1)} all-to-all(f32[2,32,32,128]{3,2,0,1:T(8,128)S(1)} %copy.28), channel_id=1, replica_groups=mesh['row'=16,'col'=32] {'col'}, dimensions={1} | all-to-all | bytes 2097152 | tf_op jit(solution)/shard_map/all_to_all | solution.py:65
  149.0 35.6 %all_to_all.40 = f32[2,2,16,32,128]{4,3,1,0,2:T(8,128)S(1)} all-to-all(f32[2,2,16,32,128]{4,3,1,0,2:T(8,128)S(1)} %copy.29), channel_id=1, replica_groups=mesh['row'=16,'col'=32] {'row'}, dimensions={2} | all-to-all | bytes 2097152 | tf_op jit(solution)/shard_map/all_to_all | solution.py:69
  184.7 148.5 %all-reduce.3.cloned.1.call-done = f32[128,128]{1,0:T(8,128)} async-done(((f32[128,128]{1,0:T(8,128)}), f32[128,128]{1,0:T(8,128)}) %all-reduce.3.cloned.1.call-update) | async-done | bytes 65552 | tf_op jit(solution)/shard_map/psum | solution.py:25
  333.2 1.1 fusion.73
  334.3 1.5 fusion.83
  335.8 34.1 %all_gather.14 = bf16[2,2,16,1,32,128]{5,4,3,1,0,2:T(8,128)(2,1)S(1)} all-gather(bf16[2,2,1,1,32,128]{5,4,3,1,0,2:T(8,128)(2,1)} %bitcast.234), channel_id=1, replica_groups=mesh['row'=16,'col'=32] {'row'}, dimensions={2}, use_global_device_ids=true | all-gather | bytes 557056 | tf_op jit(solution)/shard_map/all_gather | solution.py:26
  369.9 0.9 copy.33
  370.8 10.8 %all-to-all-start.3 = ((bf16[2,32,1,32,128]{4,3,0,2,1:T(8,128)(2,1)}), bf16[2,32,1,32,128]{4,3,0,2,1:T(8,128)(2,1)S(1)}, u32[]{:S(2)}, u32[]{:S(2)}) async-start(bf16[2,32,1,32,128]{4,3,0,2,1:T(8,128)(2,1)} %copy.33), calls=%async_computation.4 | async-start | bytes 1048576 | tf_op jit(solution)/shard_map/all_to_all | solution.py:28
  381.7 0.8 convolution_bitcast_fusion
  382.5 16.3 %all-to-all-done.3 = bf16[2,32,1,32,128]{4,3,0,2,1:T(8,128)(2,1)S(1)} async-done(((bf16[2,32,1,32,128]{4,3,0,2,1:T(8,128)(2,1)}), bf16[2,32,1,32,128]{4,3,0,2,1:T(8,128)(2,1)S(1)}, u32[]{:S(2)}, u32[]{:S(2)}) %all-to-all-start.3) | async-done | bytes 524320 | tf_op jit(solution)/shard_map/all_to_all | solution.py:28
  398.8 0.8 copy.34
  399.6 2.3 copy.36
  402.2 28.4 %while.31 = (s32[]{:T(128)}, f32[4,1024,128]{2,1,0:T(8,128)S(1)}, f32[2,1024,128]{2,1,0:T(8,128)S(1)}, s32[]{:T(128)}, s32[2,2]{1,0:T(2,128)S(1)}, /*index=5*/bf...) while((s32[]{:T(128)}, f32[4,1024,128]{2,1,0:T(8,128)S(1)}, ...), condition=%wide.region_6.7_spmd, body=%wide.region_5.6_spmd.sunk | while | flops 537264128 | bytes 11010713 | solution.py:56
  402.8 0.6 fusion.116
  408.7 0.9 constant_dynamic-slice_fusion.13
  409.6 0.3 copy-done
  409.9 2.3 fusion.117
  413.5 2.5 fusion.118
  416.7 0.6 fusion.116
  422.6 0.9 constant_dynamic-slice_fusion.13
  423.5 0.3 copy-done
  423.8 2.3 fusion.117
  427.4 2.5 fusion.118
  430.6 1.6 copy.37
  432.3 32.5 %all_to_all.39 = f32[2,32,32,128]{3,2,0,1:T(8,128)S(1)} all-to-all(f32[2,32,32,128]{3,2,0,1:T(8,128)S(1)} %copy.38), channel_id=1, replica_groups=mesh['row'=16,'col'=32] {'col'}, dimensions={1} | all-to-all | bytes 2097152 | tf_op jit(solution)/shard_map/all_to_all | solution.py:65
  464.9 33.4 %all_to_all.41 = f32[2,2,16,32,128]{4,3,1,0,2:T(8,128)S(1)} all-to-all(f32[2,2,16,32,128]{4,3,1,0,2:T(8,128)S(1)} %copy.39), channel_id=1, replica_groups=mesh['row'=16,'col'=32] {'row'}, dimensions={2} | all-to-all | bytes 2097152 | tf_op jit(solution)/shard_map/all_to_all | solution.py:69
  498.4 148.5 %all-reduce.5.cloned.1.call-done = f32[128,128]{1,0:T(8,128)} async-done(((f32[128,128]{1,0:T(8,128)}), f32[128,128]{1,0:T(8,128)}) %all-reduce.5.cloned.1.call-update) | async-done | bytes 65552 | tf_op jit(solution)/shard_map/psum | solution.py:25
  646.9 1.7 fusion.68
  (44 shorter events, 1.2 us)
Async XLA Ops:
  7.4 78.0 %all-gather.3.cloned.1.call-start = ((), (), s32[]{:S(2)}) async-start(), calls=%async_computation.8 | async-start | bytes 1081344 | tf_op jit(solution)/shard_map/all_gather | solution.py:23
  8.8 57.6 %copy-start.5 = (bf16[2,2,1,1,32,128]{5,4,3,2,1,0:T(8,128)(2,1)S(1)}, bf16[2,2,1,1,32,128]{5,4,3,2,1,0:T(8,128)(2,1)}, u32[]{:S(2)}) copy-start(bf16[2,2,1,1,32,128]{5,4,3,2,1,0:T(8,128)(2,1)} %convert_element_type.22) | copy-start | bytes 98308
  47.8 36.7 %all-to-all-start = ((bf16[2,32,1,32,128]{4,3,0,2,1:T(8,128)(2,1)}), bf16[2,32,1,32,128]{4,3,0,2,1:T(8,128)(2,1)S(1)}, u32[]{:S(2)}, u32[]{:S(2)}) async-start(bf16[2,32,1,32,128]{4,3,0,2,1:T(8,128)(2,1)} %bitcast.20), calls=%async_computation | async-start | bytes 1048576 | tf_op jit(solution)/shard_map/all_to_all | solution.py:28
  66.3 266.9 %all-reduce.3.cloned.1.call-start = ((), (), s32[]{:S(2)}) async-start(), calls=%async_computation.10 | async-start | bytes 131072 | tf_op jit(solution)/shard_map/psum | solution.py:25
  67.2 266.0 %reduce-scatter.3.cloned.1.call-start = ((), (), s32[]{:S(2)}) async-start(), calls=%async_computation.9 | async-start | bytes 2162688 | tf_op jit(solution)/shard_map/reduce_scatter | solution.py:62
  67.3 18.3 %copy-start.6 = (s32[2,2]{1,0:T(2,128)S(1)}, s32[2,2]{1,0:T(2,128)}, u32[]{:S(2)}) copy-start(s32[2,2]{1,0:T(2,128)} %param.9) | copy-start | bytes 52
  92.2 1.2 copy-start.1
  106.2 1.2 copy-start.1
  115.8 283.8 %all-gather.5.cloned.1.call-start = ((), (), s32[]{:S(2)}) async-start(), calls=%async_computation.11 | async-start | bytes 1081344 | tf_op jit(solution)/shard_map/all_gather | solution.py:23
  148.9 184.3 %copy-start.2 = (f32[2,2,1,1,32,128]{5,4,3,2,1,0:T(8,128)S(1)}, f32[2,2,1,1,32,128]{5,4,3,2,1,0:T(8,128)}, u32[]{:S(2)}) copy-start(f32[2,2,1,1,32,128]{5,4,3,2,1,0:T(8,128)} %param.11) | copy-start | bytes 196612
  335.8 45.9 %copy-start.4 = (bf16[2,2,1,1,32,128]{5,4,1,0,3,2:T(8,128)(2,1)S(1)}, bf16[2,2,1,1,32,128]{5,4,1,0,3,2:T(8,128)(2,1)}, u32[]{:S(2)}) copy-start(bf16[2,2,1,1,32,128]{5,4,1,0,3,2:T(8,128)(2,1)} %fusion.83) | copy-start | bytes 98308
  370.8 28.0 %all-to-all-start.3 = ((bf16[2,32,1,32,128]{4,3,0,2,1:T(8,128)(2,1)}), bf16[2,32,1,32,128]{4,3,0,2,1:T(8,128)(2,1)S(1)}, u32[]{:S(2)}, u32[]{:S(2)}) async-start(bf16[2,32,1,32,128]{4,3,0,2,1:T(8,128)(2,1)} %copy.33), calls=%async_computation.4 | async-start | bytes 1048576 | tf_op jit(solution)/shard_map/all_to_all | solution.py:28
  381.6 265.3 %all-reduce.5.cloned.1.call-start = ((), (), s32[]{:S(2)}) async-start(), calls=%async_computation.13 | async-start | bytes 131072 | tf_op jit(solution)/shard_map/psum | solution.py:25
  382.5 264.4 %reduce-scatter.5.cloned.1.call-start = ((), (), s32[]{:S(2)}) async-start(), calls=%async_computation.12 | async-start | bytes 2162688 | tf_op jit(solution)/shard_map/reduce_scatter | solution.py:62
  408.7 1.2 copy-start
  422.6 1.2 copy-start
  464.9 182.0 %copy-start.3 = (f32[2,2,1,32,128]{4,3,1,0,2:T(8,128)S(1)}, f32[2,2,1,32,128]{4,3,1,0,2:T(8,128)}, u32[]{:S(2)}) copy-start(f32[2,2,1,32,128]{4,3,1,0,2:T(8,128)} %reduce-scatter.3.cloned.1.call-done) | copy-start | bytes 196612
Sparse Core Ops, SparseCore 0:
  10.3 73.8 all-gather.2
  115.9 122.2 reduce-scatter.2
  335.9 60.5 all-gather.4
  432.3 120.5 reduce-scatter.4
Sparse Core Ops, SparseCore 1:
  72.6 260.6 all-reduce.2
  387.1 259.8 all-reduce.4
where the time goes:
time: 657 us; the launch traced here: 656 us
  waiting for transfers between devices  331 us (50%)
  blocking collectives  207 us (32%)
  loops' own time  30.4 us (5%)
  starting transfers between devices  29.5 us (4%)
  matrix products  23.7 us (4%)
  local copies, waits for them, and re-layouts  17 us (3%)
  between operations  14.7 us (2%)
    psum x2, waiting for transfers between devices, shards(): lax.psum(self_gram(halves.reshape(-1, rank_width)), ('row', 'col'))  297 us
    all_gather x2, blocking collectives, shards(): spread = lax.all_gather(halves, 'row', axis=2, tiled=True)  72.1 us
    all_to_all x2, blocking collectives, shards(): lax.all_to_all(moved_pieces, 'row', split_axis=2, concat_axis=2, tiled=True)  69.1 us
    all_to_all x2, blocking collectives, shards(): lax.all_to_all(pieces, 'col', split_axis=1, concat_axis=1, tiled=True)  65.4 us
    all_to_all x2, waiting for transfers between devices, shards(): lax.all_to_all(spread, 'col', split_axis=1, concat_axis=2, tiled=True)  33.5 us
    another operation x2, loops' own time, shards(): lax.fori_loop(0, tile_count[0], add_tile, (row_start, column_start))  30.4 us
    all_to_all x2, starting transfers between devices, shards(): lax.all_to_all(spread, 'col', split_axis=1, concat_axis=2, tiled=True)  29.3 us
  transfers between devices with their start and end apart: 8, of which 4 were waited for; matrix products, arithmetic and copies ran while one was open for 6% of the time, Pallas kernels for 0%

commit v1 on v0

v1 whole, which is shorter than its diff:
```python
import jax
import jax.numpy as jnp
from jax import lax
from jax.experimental import pallas as pl
from jax.experimental.pallas import tpu as pltpu
from jax.sharding import PartitionSpec as P

ITERS = 2
MESH = pl.DeviceIdType.MESH
F32 = jnp.float32
BF16 = jnp.bfloat16
N_KEYS = 112
LAST = (4, 3)


def kernel(
    blocks, count, tiles_hbm, f_ref, o_ref,
    tiles, rp, cp, rs, cr, zb, cs, yb, xs, xr, fr, gm, gr, gf, terms,
    tile_sem, send_sem, recv_sem, gram_send, gram_recv,
):
    r = lax.axis_index("row")
    c = lax.axis_index("col")
    xh, y = r // 8, r % 8
    z, q = c // 4, c % 4
    xi, ka = q // 2, q % 2

    def spread(t):
        return (t % 8 + (1 + 3 * (t // 4) + 2 * (t % 4)) % 4) % 8

    holder_y = (z + 2 * q + spread(r)) % 8
    holders = [[(h * 8 + holder_y, r + 16 * k) for h in range(2)] for k in range(2)]
    owner_row = c % 16
    column_k = c // 16
    shift = spread(owner_row)
    owner_z = [(y + 16 - 2 * w - shift) % 8 for w in range(4)]
    owners = [(owner_row, owner_z[w] * 4 + w) for w in range(4)]

    core_peer = (r, z * 4 + xi * 2 + (1 - ka))
    x_peer = (r, z * 4 + (1 - xi) * 2 + ka)
    z_next = [(r, ((z + 1) % 8) * 4 + q), (r, ((z + 7) % 8) * 4 + q)]
    y_next = [(xh * 8 + (y + 1) % 8, c), (xh * 8 + (y + 7) % 8, c)]

    tile_copy = pltpu.make_async_copy(tiles_hbm, tiles, tile_sem)
    tile_copy.start()

    barrier = pltpu.get_barrier_semaphore()
    near = [core_peer, x_peer] + z_next + holders[0] + holders[1] + owners
    for device in near:
        pl.semaphore_signal(barrier, inc=1, device_id=device, device_id_type=MESH)

    def greet(d, carry):
        pl.semaphore_signal(barrier, inc=1, device_id=((r + d) % 16, c), device_id_type=MESH)
        return carry

    lax.fori_loop(1, 16, greet, 0)
    o_ref[...] = f_ref[...]
    pl.semaphore_wait(barrier, len(near) + 15)

    def chunk_of(pos, direction, slot):
        return (pos + 3 - slot) % 8 if direction == 0 else (pos + 6 + slot) % 8

    def sweep(it, carry):
        keys = {}
        sends = []

        def number(key):
            return keys.setdefault(key, len(keys))

        def push(key, src, dst, device):
            n = number(key)
            copy = pltpu.make_async_remote_copy(
                src_ref=src, dst_ref=dst, send_sem=send_sem.at[n], recv_sem=recv_sem.at[it, n],
                device_id=device, device_id_type=MESH,
            )
            copy.start()
            sends.append(copy)

        def arrived(key, dst):
            n = number(key)
            pltpu.make_async_remote_copy(
                src_ref=dst, dst_ref=dst, send_sem=send_sem.at[n], recv_sem=recv_sem.at[it, n],
                device_id=core_peer, device_id_type=MESH,
            ).wait_recv()

        rp[it, z, xi, ka] = o_ref[...].astype(BF16)
        mine = rp.at[it, z, xi, ka]
        for k in range(2):
            for h in range(2):
                n = number(("scatter", k, h))
                copy = pltpu.make_async_remote_copy(
                    src_ref=rp.at[it, z, xi, ka, :, k], dst_ref=cp.at[it, holder_y, q],
                    send_sem=send_sem.at[n], recv_sem=recv_sem.at[it, N_KEYS - 4 + q],
                    device_id=holders[k][h], device_id_type=MESH,
                )
                copy.start()
                sends.append(copy)

        def chain(h):
            return xi if h == 0 else 1 - xi

        def row_piece(pos, h):
            return rp.at[it, pos, chain(h), ka]

        def column_piece(pos, h):
            return cp.at[it, pos, 2 * h:2 * h + 2]

        def pass_row(direction, step, h):
            pos = (z + 8 - step) % 8 if direction == 0 else (z + step) % 8
            piece = row_piece(pos, h)
            if step > 0:
                arrived(("zg", direction, step, h), piece)
            if step < LAST[direction]:
                push(("zg", direction, step + 1, h), piece, piece, z_next[direction])
            if step > 0 or direction == 0:
                push(("cg", direction, step, h), piece, piece, core_peer)

        def pass_column(direction, step, h):
            pos = (y + 8 - step) % 8 if direction == 0 else (y + step) % 8
            piece = column_piece(pos, h)
            if step > 0:
                arrived(("yg", direction, step, h), piece)
            if step < LAST[direction]:
                push(("yg", direction, step + 1, h), piece, piece, y_next[direction])

        push(("x",), mine, mine, x_peer)
        for direction in range(2):
            pass_row(direction, 0, 0)
        arrived(("x",), row_piece(z, 1))
        for direction in range(2):
            pass_row(direction, 0, 1)
        for h in range(2):
            for w in (2 * h, 2 * h + 1):
                pltpu.make_async_remote_copy(
                    src_ref=cp.at[it, y, w], dst_ref=cp.at[it, y, w],
                    send_sem=send_sem.at[0], recv_sem=recv_sem.at[it, N_KEYS - 4 + w],
                    device_id=core_peer, device_id_type=MESH,
                ).wait_recv()
            for direction in range(2):
                pass_column(direction, 0, h)
        for step in range(1, 5):
            for h in range(2):
                for direction in range(2):
                    if step <= LAST[direction]:
                        pass_row(direction, step, h)
                        pass_column(direction, step, h)
        for step in range(0, 5):
            for h in range(2):
                for direction in range(2):
                    if step <= LAST[direction] and (step > 0 or direction == 0):
                        pos = (z + 8 - step) % 8 if direction == 0 else (z + step) % 8
                        arrived(("cg", direction, step, h), rp.at[it, pos, chain(h), 1 - ka])

        @pl.when(it == 0)
        def _():
            tile_copy.wait()

        live = [(count[0] > s).astype(F32) for s in range(2)]
        off = [(blocks[s, 0] != blocks[s, 1]).astype(F32) for s in range(2)]
        row_slot = [blocks[s, 0] // 16 for s in range(2)]
        column_slot = [blocks[s, 1] // 32 for s in range(2)]

        for s in range(2):
            left = rp[it, :, :, :, row_slot[s] // 2, row_slot[s] % 2].reshape(1024, 128).T
            for n in range(4):
                term = jnp.dot(left, tiles[s, :, n * 256:(n + 1) * 256], preferred_element_type=F32)
                terms[s, n * 256:(n + 1) * 256, :] = term.T
        for p in range(2):
            weight = [live[s] * off[s] * (column_slot[s] == p).astype(F32) for s in range(2)]
            for v in range(32):
                rows = slice(v * 32, v * 32 + 32)
                cs[it, (v // 4 + 2 * (v % 4) + shift) % 8, v % 4, p] = (
                    weight[0] * terms[0, rows] + weight[1] * terms[1, rows]
                )

        def column_sum(pos, h):
            return cs.at[it, pos, 2 * h:2 * h + 2]

        for h in range(2):
            for direction, far in ((0, 4), (1, 5)):
                push(
                    ("yr", direction, 0, h), column_sum((y + far) % 8, h),
                    yb.at[it, direction, 0, h], y_next[direction],
                )

        for s in range(2):
            right = jnp.concatenate(
                [
                    cp[it, (v // 4 + 2 * (v % 4) + shift) % 8, v % 4, column_slot[s]]
                    for v in range(32)
                ],
                axis=0,
            )
            for n in range(4):
                rows = slice(n * 256, (n + 1) * 256)
                terms[s, rows, :] = jnp.dot(tiles[s, rows, :], right, preferred_element_type=F32)
        for slot in range(4):
            weight = [live[s] * (row_slot[s] == slot).astype(F32) for s in range(2)]
            both = weight[0] * terms[0] + weight[1] * terms[1]
            rs[it, :, :, :, slot // 2, slot % 2] = both.reshape(8, 2, 2, 32, 128)

        order = (4, 5, 3, 6, 2, 7, 1, 0)
        for far in order:
            pos = (z + far) % 8
            push(("cr", far), rs.at[it, pos, :, 1 - ka], cr.at[it, pos], core_peer)

        total = jnp.zeros((128, 128), F32)
        for slot in range(4):
            panel = rp[it, :, :, :, slot // 2, slot % 2].reshape(1024, 128)
            total = total + jnp.dot(panel.T, panel, preferred_element_type=F32)
        gm[it] = total.reshape(16, 8, 128)

        def gram_scatter(d, carry):
            pltpu.make_async_remote_copy(
                src_ref=gm.at[it, (r + d) % 16], dst_ref=gr.at[it, d - 1],
                send_sem=gram_send.at[0], recv_sem=gram_recv.at[it, 0],
                device_id=((r + d) % 16, c), device_id_type=MESH,
            ).start()
            return carry

        def gram_gather(d, carry):
            pltpu.make_async_remote_copy(
                src_ref=gf.at[it, r], dst_ref=gf.at[it, r],
                send_sem=gram_send.at[1], recv_sem=gram_recv.at[it, 1],
                device_id=((r + d) % 16, c), device_id_type=MESH,
            ).start()
            return carry

        def bytes_of_fifteen(sem):
            pltpu.make_async_copy(gr.at[it], gr.at[it], sem).wait()

        lax.fori_loop(1, 16, gram_scatter, 0)

        def own_row(pos, h):
            return rs[it, pos, h, ka] + cr[it, pos, h]

        def pass_row_sum(direction, slot, h):
            pos = chunk_of(z, direction, slot)
            buf = zb.at[it, direction, slot, h]
            arrived(("zr", direction, slot, h), buf)
            if h == 0:
                arrived(("cr", (3 - slot) if direction == 0 else (6 + slot)), cr.at[it, pos])
            zb[it, direction, slot, h] += own_row(pos, h)
            push(("zr", direction, slot + 1, h), buf, zb.at[it, direction, slot + 1, h], z_next[direction])

        def pass_column_sum(direction, slot, h):
            pos = chunk_of(y, direction, slot)
            buf = yb.at[it, direction, slot, h]
            arrived(("yr", direction, slot, h), buf)
            yb[it, direction, slot, h] += cs[it, pos, 2 * h:2 * h + 2]
            push(("yr", direction, slot + 1, h), buf, yb.at[it, direction, slot + 1, h], y_next[direction])

        for direction, far in ((0, 4), (1, 5)):
            pos = (z + far) % 8
            arrived(("cr", far), cr.at[it, pos])
            for h in range(2):
                rs[it, pos, h, ka] = own_row(pos, h)
                push(
                    ("zr", direction, 0, h), rs.at[it, pos, h, ka],
                    zb.at[it, direction, 0, h], z_next[direction],
                )
        for slot in range(3):
            for h in range(2):
                for direction in range(2):
                    if slot < LAST[direction] - 1:
                        pass_column_sum(direction, slot, h)
                        pass_row_sum(direction, slot, h)
            if slot == 0:
                bytes_of_fifteen(gram_recv.at[it, 0])
                gf[it, r] = gm[it, r] + jnp.sum(gr[it], axis=0)
                lax.fori_loop(1, 16, gram_gather, 0)

        for h in range(2):
            for direction in range(2):
                slot = LAST[direction] - 1
                arrived(("yr", direction, slot, h), yb.at[it, direction, slot, h])
            yb[it, 0, 3, h] += cs[it, y, 2 * h:2 * h + 2] + yb[it, 1, 2, h]
            for w in range(2):
                n = number(("owner", 2 * h + w))
                copy = pltpu.make_async_remote_copy(
                    src_ref=yb.at[it, 0, 3, h, w], dst_ref=fr.at[it, column_k, xh],
                    send_sem=send_sem.at[n], recv_sem=recv_sem.at[it, N_KEYS - 8 + column_k * 2 + xh],
                    device_id=owners[2 * h + w], device_id_type=MESH,
                )
                copy.start()
                sends.append(copy)
        arrived(("cr", 0), cr.at[it, z])
        for h in range(2):
            for direction in range(2):
                slot = LAST[direction] - 1
                arrived(("zr", direction, slot, h), zb.at[it, direction, slot, h])
            xs[it, h] = own_row(z, h) + zb[it, 0, 3, h] + zb[it, 1, 2, h]
        push(("xr",), xs.at[it, 1 - xi], xr.at[it], x_peer)

        bytes_of_fifteen(gram_recv.at[it, 1])
        held = o_ref[...]
        below = jnp.dot(
            held.reshape(128, 128), gf[it].reshape(128, 128),
            precision=lax.Precision.HIGHEST, preferred_element_type=F32,
        ).reshape(2, 2, 32, 128)
        arrived(("xr",), xr.at[it])
        for k in range(2):
            for h in range(2):
                pltpu.make_async_remote_copy(
                    src_ref=fr.at[it, k, h], dst_ref=fr.at[it, k, h],
                    send_sem=send_sem.at[0], recv_sem=recv_sem.at[it, N_KEYS - 8 + k * 2 + h],
                    device_id=core_peer, device_id_type=MESH,
                ).wait_recv()
        product = xs[it, xi] + xr[it]
        for k in range(2):
            above = product[:, k] + (fr[it, k, 0] + fr[it, k, 1])
            o_ref[:, k] = held[:, k] * (0.5 + 0.5 * above / below[:, k])

        for copy in sends:
            copy.wait_send()
        for phase in range(2):
            bytes_of_fifteen(gram_send.at[phase])
        assert len(keys) <= N_KEYS - 8
        return carry

    lax.fori_loop(0, ITERS, sweep, 0)


def shards(tiles, tile_blocks, tile_count, factor):
    vmem = pl.BlockSpec(memory_space=pltpu.VMEM)
    smem = pl.BlockSpec(memory_space=pltpu.SMEM)
    held = pl.pallas_call(
        kernel,
        out_shape=jax.ShapeDtypeStruct((2, 2, 32, 128), F32),
        in_specs=[smem, smem, pl.BlockSpec(memory_space=pl.ANY), vmem],
        out_specs=vmem,
        scratch_shapes=[
            pltpu.VMEM((2, 1024, 1024), BF16),
            pltpu.VMEM((2, 8, 2, 2, 2, 2, 32, 128), BF16),
            pltpu.VMEM((2, 8, 4, 2, 32, 128), BF16),
            pltpu.VMEM((2, 8, 2, 2, 2, 2, 32, 128), F32),
            pltpu.VMEM((2, 8, 2, 2, 2, 32, 128), F32),
            pltpu.VMEM((2, 2, 4, 2, 2, 2, 32, 128), F32),
            pltpu.VMEM((2, 8, 4, 2, 32, 128), F32),
            pltpu.VMEM((2, 2, 4, 2, 2, 2, 32, 128), F32),
            pltpu.VMEM((2, 2, 2, 2, 32, 128), F32),
            pltpu.VMEM((2, 2, 2, 32, 128), F32),
            pltpu.VMEM((2, 2, 2, 2, 32, 128), F32),
            pltpu.VMEM((2, 16, 8, 128), F32),
            pltpu.VMEM((2, 15, 8, 128), F32),
            pltpu.VMEM((2, 16, 8, 128), F32),
            pltpu.VMEM((2, 1024, 128), F32),
            pltpu.SemaphoreType.DMA,
            pltpu.SemaphoreType.DMA((N_KEYS,)),
            pltpu.SemaphoreType.DMA((2, N_KEYS)),
            pltpu.SemaphoreType.DMA((2,)),
            pltpu.SemaphoreType.DMA((2, 2)),
        ],
        compiler_params=pltpu.CompilerParams(
            collective_id=0, has_side_effects=True, vmem_limit_bytes=50 * 1024 * 1024
        ),
    )(tile_blocks, tile_count, tiles, factor.reshape(2, 2, 32, 128))
    return held.reshape(factor.shape)


def solution(mesh):
    in_specs = (
        P(("row", "col"), None, None),
        P(("row", "col"), None),
        P(("row", "col")),
        P(None, None, "row", "col", None, None),
    )
    out_specs = P(None, None, "row", "col", None, None)
    return jax.shard_map(shards, mesh=mesh, in_specs=in_specs, out_specs=out_specs, check_vma=False)
```

time: 657 us -> 130 us (0.20)
  waiting for transfers between devices: 331 us -> 0 us
  blocking collectives: 207 us -> 0 us
  Pallas kernels: 0 us -> 125 us
  loops' own time: 30.4 us -> 0 us
  starting transfers between devices: 29.5 us -> 0 us
  matrix products: 23.7 us -> 0 us
  local copies, waits for them, and re-layouts: 17 us -> 2.14 us
  between operations: 14.7 us -> 0.67 us
    psum x2 -> x0, waiting for transfers between devices: 297 us -> none  [shards(): lax.psum(self_gram(halves.reshape(-1, rank_width)), ('row', 'col'))]
    all_to_all x4 -> x0, blocking collectives: 134 us -> none  [the longest x2 69.1 us: shards(): lax.all_to_all(moved_pieces, 'row', split_axis=2, concat_axis=2, tiled=True)]
    pallas_call x0 -> x1, Pallas kernels: none -> 125 us  [shards(): pl.pallas_call(kernel, out_shape=jax.ShapeDtypeStruct((2, 2, 32, 128), F3...]
    all_gather x2 -> x0, blocking collectives: 72.1 us -> none  [shards(): spread = lax.all_gather(halves, 'row', axis=2, tiled=True)]
    all_to_all x2 -> x0, waiting for transfers between devices: 33.5 us -> none  [shards(): lax.all_to_all(spread, 'col', split_axis=1, concat_axis=2, tiled=True)]
    another operation x2 -> x0, loops' own time: 30.4 us -> none  [shards(): lax.fori_loop(0, tile_count[0], add_tile, (row_start, column_start))]
    all_to_all x2 -> x0, starting transfers between devices: 29.3 us -> none  [shards(): lax.all_to_all(spread, 'col', split_axis=1, concat_axis=2, tiled=True)]
    dot_general x12 -> x0, matrix products: 23.7 us -> none  [the longest x4 10.1 us: add_tile(): lax.dot_general(block_tile, left_rows, (((0,), (0,)), ((), ())), preferre...]
  transfers between devices with their start and end apart: 8 -> 0, of which waited for: 4 -> 0; matrix products, arithmetic and copies ran while one was open for 6% -> 0% of each run, Pallas kernels for 0% -> 0%
where the time goes in v1:
time: 130 us; the launch traced here: 128 us
  Pallas kernels  125 us (96%)
  local copies, waits for them, and re-layouts  2.14 us (2%)
    pallas_call x1, Pallas kernels, shards(): pl.pallas_call(kernel, out_shape=jax.ShapeDtypeStruct((2, 2, 32, 128), F3...  125 us

profile of v1, /device:TPU:1, one launch (start us, length us, event | category | flops | bytes accessed | tf_op | source)
XLA Modules:
  0.0 128.0 jit_solution(7402116106779239780)
XLA Ops:
  0.7 0.0 copy-start
  0.7 0.8 copy-done
  1.5 0.0 copy-start.1
  1.5 0.7 copy-done.1
  2.2 125.2 %shard_map.46 = f32[2,2,32,128]{3,2,1,0:T(8,128)S(1)} custom-call(s32[2,2]{1,0:T(2,128)S(1)} %copy-done.1, s32[1]{0:T(128)S(6)} %copy.7.count, bf16[2,1024,1024]{2,1,0:T(8,128)(2,1)} %tiles_hbm.1, f32[2,2,32,128]{3,2,1,0:T(8,128)S(1)} %bitcast.5), custom_call_target="tpu_custom_call" | custom-call | tf_op jit(solution)/shard_map/pallas_call | solution.py:326
  127.4 0.6 copy.8
Async XLA Ops:
  0.7 0.8 copy-start
  1.5 0.7 copy-start.1

commit v2 on v1

v2 whole, which is shorter than its diff:
```python
import jax
import jax.numpy as jnp
from jax import lax
from jax.experimental import pallas as pl
from jax.experimental.pallas import tpu as pltpu
from jax.sharding import PartitionSpec as P

ITERS = 2
MESH = pl.DeviceIdType.MESH
F32 = jnp.float32
BF16 = jnp.bfloat16
N_KEYS = 112


def hops(direction, h):
    return 4 if direction == h else 3


def kernel(
    blocks, count, tiles_hbm, f_ref, o_ref,
    tiles, rp, cp, rs, cr, zb, cs, yb, xs, xr, fr, gm, gr, gf, terms, right, yo, fa, fm,
    tile_sem, send_sem, recv_sem, gram_send, gram_recv,
):
    r = lax.axis_index("row")
    c = lax.axis_index("col")
    xh, y = r // 8, r % 8
    z, q = c // 4, c % 4
    xi, ka = q // 2, q % 2

    def spread(t):
        b3, b2, b1, b0 = t // 8, (t // 4) % 2, (t // 2) % 2, t % 2
        return ((2 * b1 + 2 * b3 + 1 - b2 + b0 + 2 * b2 * b0) % 4 + 4 * b2) % 8

    holder_y = (z + 2 * q + spread(r)) % 8
    holders = [[(h * 8 + holder_y, r + 16 * k) for h in range(2)] for k in range(2)]
    owner_row = c % 16
    column_k = c // 16
    shift = spread(owner_row)
    owner_z = [(y + 16 - 2 * w - shift) % 8 for w in range(4)]
    owners = [(owner_row, owner_z[w] * 4 + w) for w in range(4)]

    stations = [
        ((owner_row // 8) * 8 + y, owner_z[w] * 4 + (1 - xi) * 2 + 1 - w % 2) for w in range(4)
    ]
    my_station = (xh * 8 + holder_y, z * 4 + (1 - (r // 2) % 2) * 2 + 1 - ka)
    base = (y + 24 - z - 2 * (1 - ka) - 2 * (1 - xi) - 2 * xh) % 4
    served_row = 8 * xh + 4 * (1 - ((base + 1) % 4) // 2) + 2 * (1 - xi) + base // 2
    served = (served_row, z * 4 + ((y + 16 - z - spread(served_row)) % 8) // 2)
    feeders = [(h * 8 + y, served_row + 16 * k) for k in range(2) for h in range(2)]

    core_peer = (r, z * 4 + xi * 2 + (1 - ka))
    x_peer = (r, z * 4 + (1 - xi) * 2 + ka)
    z_next = [(r, ((z + 1) % 8) * 4 + q), (r, ((z + 7) % 8) * 4 + q)]
    y_next = [(xh * 8 + (y + 1) % 8, c), (xh * 8 + (y + 7) % 8, c)]

    tile_copy = pltpu.make_async_copy(tiles_hbm, tiles, tile_sem)
    tile_copy.start()

    barrier = pltpu.get_barrier_semaphore()
    near = [core_peer, x_peer] + z_next + owners + feeders + [my_station]
    for device in near:
        pl.semaphore_signal(barrier, inc=1, device_id=device, device_id_type=MESH)

    def greet(d, carry):
        pl.semaphore_signal(barrier, inc=1, device_id=((r + d) % 16, c), device_id_type=MESH)
        return carry

    lax.fori_loop(1, 16, greet, 0)
    o_ref[...] = f_ref[...]
    pl.semaphore_wait(barrier, len(near) + 15)

    def source_of(pos, direction, step):
        return (pos + 8 - step) % 8 if direction == 0 else (pos + step) % 8

    def sweep(it, carry):
        keys = {}
        sends = []

        def number(key):
            return keys.setdefault(key, len(keys))

        def push(key, src, dst, device):
            n = number(key)
            copy = pltpu.make_async_remote_copy(
                src_ref=src, dst_ref=dst, send_sem=send_sem.at[n], recv_sem=recv_sem.at[it, n],
                device_id=device, device_id_type=MESH,
            )
            copy.start()
            sends.append(copy)

        def arrived(key, dst):
            n = number(key)
            pltpu.make_async_remote_copy(
                src_ref=dst, dst_ref=dst, send_sem=send_sem.at[n], recv_sem=recv_sem.at[it, n],
                device_id=core_peer, device_id_type=MESH,
            ).wait_recv()

        rp[it, z, xi, ka] = o_ref[...].astype(BF16)
        mine = rp.at[it, z, xi, ka]
        for k in range(2):
            for h in range(2):
                n = number(("scatter", k, h))
                copy = pltpu.make_async_remote_copy(
                    src_ref=rp.at[it, z, xi, ka, :, k], dst_ref=cp.at[it, holder_y, q],
                    send_sem=send_sem.at[n], recv_sem=recv_sem.at[it, N_KEYS - 4 + q],
                    device_id=holders[k][h], device_id_type=MESH,
                )
                copy.start()
                sends.append(copy)

        def chain(h):
            return xi if h == 0 else 1 - xi

        def row_piece(pos, h):
            return rp.at[it, pos, chain(h), ka]

        def column_piece(pos, h):
            return cp.at[it, pos, 2 * h:2 * h + 2]

        def pass_row(direction, step, h):
            pos = source_of(z, direction, step)
            piece = row_piece(pos, h)
            if step > 0:
                arrived(("zg", direction, step, h), piece)
            if step < hops(direction, h):
                push(("zg", direction, step + 1, h), piece, piece, z_next[direction])

        def pass_column(direction, step, h):
            piece = column_piece(source_of(y, direction, step), h)
            if step > 0:
                arrived(("yg", direction, step, h), piece)
            if step < hops(direction, h):
                push(("yg", direction, step + 1, h), piece, piece, y_next[direction])

        def directions(step):
            return (0, 1) if 0 < step < 4 else (0,)

        def across(step):
            for direction in directions(step):
                pieces = rp.at[it, source_of(z, direction, step), :, ka]
                push(("cg", direction, step), pieces, pieces, core_peer)

        def each(passing, step):
            for h in range(2):
                for direction in range(2):
                    if step <= hops(direction, h):
                        passing(direction, step, h)

        live = [(count[0] > s).astype(F32) for s in range(2)]
        off = [(blocks[s, 0] != blocks[s, 1]).astype(F32) for s in range(2)]
        row_slot = [blocks[s, 0] // 16 for s in range(2)]
        is_row = [[(row_slot[s] == slot).astype(F32) for slot in range(4)] for s in range(2)]
        column_slot = [blocks[s, 1] // 32 for s in range(2)]

        def tile_rows(s, pos, columns):
            return tiles[s, pl.ds(pl.multiple_of(pos * 128, 128), 128), columns]

        def joined(parts):
            return parts[0] if len(parts) == 1 else jnp.concatenate(parts, axis=0)

        def chosen(s, pos):
            total = None
            for slot in range(4):
                part = is_row[s][slot] * rp[it, pos, :, :, slot // 2, slot % 2].astype(F32)
                total = part if total is None else total + part
            return total.reshape(128, 128).astype(BF16)

        def panel_step(step):
            for direction in directions(step):
                arrived(("cg", direction, step), rp.at[it, source_of(z, direction, step), :, 1 - ka])
            places = [source_of(z, direction, step) for direction in directions(step)]
            for s in range(2):
                left = joined([chosen(s, pos) for pos in places]).T
                for n in range(4):
                    columns = slice(n * 256, (n + 1) * 256)
                    term = jnp.dot(
                        left, joined([tile_rows(s, pos, columns) for pos in places]),
                        preferred_element_type=F32,
                    )
                    if step == 0:
                        terms[s, :, columns] = term
                    else:
                        terms[s, :, columns] += term
            total = None
            for pos in places:
                panel = rp[it, pos].reshape(512, 128)
                part = jnp.dot(panel.T, panel, preferred_element_type=F32).reshape(16, 8, 128)
                total = part if total is None else total + part
            if step == 0:
                gm[it] = total
            else:
                gm[it] += total

        push(("x",), mine, mine, x_peer)
        for direction in range(2):
            pass_row(direction, 0, 0)
        arrived(("x",), row_piece(z, 1))
        for direction in range(2):
            pass_row(direction, 0, 1)
        across(0)
        each(pass_row, 1)
        across(1)
        for h in range(2):
            for w in (2 * h, 2 * h + 1):
                pltpu.make_async_remote_copy(
                    src_ref=cp.at[it, y, w], dst_ref=cp.at[it, y, w],
                    send_sem=send_sem.at[0], recv_sem=recv_sem.at[it, N_KEYS - 4 + w],
                    device_id=core_peer, device_id_type=MESH,
                ).wait_recv()
            for direction in range(2):
                pass_column(direction, 0, h)
        each(pass_row, 2)
        across(2)
        each(pass_column, 1)

        @pl.when(it == 0)
        def _():
            tile_copy.wait()

        panel_step(0)
        each(pass_row, 3)
        across(3)
        each(pass_column, 2)
        panel_step(1)
        each(pass_row, 4)
        across(4)
        each(pass_column, 3)
        panel_step(2)
        panel_step(3)
        panel_step(4)
        for p in range(2):
            weight = [live[s] * off[s] * (column_slot[s] == p).astype(F32) for s in range(2)]
            for n in range(8):
                columns = slice(n * 128, (n + 1) * 128)
                both = (weight[0] * terms[0, :, columns] + weight[1] * terms[1, :, columns]).T
                for w in range(4):
                    cs[it, (n + 2 * w + shift) % 8, w, p] = both[w * 32:w * 32 + 32]

        def distance(direction, h, slot):
            ahead = hops(direction, h) - 1 - slot
            return ahead if direction == 0 else (8 - ahead) % 8

        chains = ((0, 0), (1, 1), (0, 1), (1, 0))
        for direction, h in chains:
            push(
                ("yr", direction, 0, h), cs.at[it, (y + distance(direction, h, -1)) % 8, 2 * h:2 * h + 2],
                yb.at[it, direction, 0, h], y_next[direction],
            )
        each(pass_column, 4)

        for s in range(2):
            for v in range(32):
                right[s, v * 32:v * 32 + 32, :] = cp[
                    it, (v // 4 + 2 * (v % 4) + shift) % 8, v % 4, column_slot[s]
                ]

        def row_chunks(fars):
            places = [(z + far) % 8 for far in fars]
            term = [
                jnp.dot(
                    joined([tile_rows(s, pos, slice(None)) for pos in places]), right[s],
                    preferred_element_type=F32,
                )
                for s in range(2)
            ]
            for slot in range(4):
                weight = [live[s] * (row_slot[s] == slot).astype(F32) for s in range(2)]
                both = weight[0] * term[0] + weight[1] * term[1]
                for n, pos in enumerate(places):
                    for w in range(4):
                        rows = slice(n * 128 + w * 32, n * 128 + w * 32 + 32)
                        rs[it, pos, w % 2, w // 2, slot // 2, slot % 2] = both[rows]
            for far, pos in zip(fars, places):
                push(("cr", far), rs.at[it, pos, 1 - ka], cr.at[it, pos], core_peer)

        row_chunks((4,))
        row_chunks((3, 5))
        met = set()

        def own_row(far, h):
            pos = (z + far) % 8
            if far not in met:
                met.add(far)
                arrived(("cr", far), cr.at[it, pos])
            return rs[it, pos, ka, h] + cr[it, pos, h]

        def own_column(far, h):
            return cs[it, (y + far) % 8, 2 * h:2 * h + 2]

        def first_sums(direction, h):
            far = distance(direction, h, -1)
            pos = (z + far) % 8
            rs[it, pos, ka, h] = own_row(far, h)
            push(
                ("zr", direction, 0, h), rs.at[it, pos, ka, h],
                zb.at[it, direction, 0, h], z_next[direction],
            )

        def pass_sums(slot):
            for direction, h in chains:
                if slot < hops(direction, h) - 1:
                    far = distance(direction, h, slot)
                    buf = yb.at[it, direction, slot, h]
                    arrived(("yr", direction, slot, h), buf)
                    yb[it, direction, slot, h] += own_column(far, h)
                    push(("yr", direction, slot + 1, h), buf, yb.at[it, direction, slot + 1, h], y_next[direction])
                    buf = zb.at[it, direction, slot, h]
                    arrived(("zr", direction, slot, h), buf)
                    zb[it, direction, slot, h] += own_row(far, h)
                    push(("zr", direction, slot + 1, h), buf, zb.at[it, direction, slot + 1, h], z_next[direction])

        for direction, h in chains:
            first_sums(direction, h)

        def gram_scatter(d, carry):
            pltpu.make_async_remote_copy(
                src_ref=gm.at[it, (r + d) % 16], dst_ref=gr.at[it, d - 1],
                send_sem=gram_send.at[0], recv_sem=gram_recv.at[it, 0],
                device_id=((r + d) % 16, c), device_id_type=MESH,
            ).start()
            return carry

        def gram_gather(d, carry):
            pltpu.make_async_remote_copy(
                src_ref=gf.at[it, r], dst_ref=gf.at[it, r],
                send_sem=gram_send.at[1], recv_sem=gram_recv.at[it, 1],
                device_id=((r + d) % 16, c), device_id_type=MESH,
            ).start()
            return carry

        def bytes_of_fifteen(sem):
            pltpu.make_async_copy(gr.at[it], gr.at[it], sem).wait()

        lax.fori_loop(1, 16, gram_scatter, 0)
        row_chunks((2, 6))
        pass_sums(0)
        row_chunks((1, 7))
        pass_sums(1)
        row_chunks((0,))
        bytes_of_fifteen(gram_recv.at[it, 0])
        gf[it, r] = gm[it, r] + jnp.sum(gr[it], axis=0)
        lax.fori_loop(1, 16, gram_gather, 0)
        pass_sums(2)

        def last_sums(box, name, h):
            total = None
            for direction in range(2):
                slot = hops(direction, h) - 1
                arrived((name, direction, slot, h), box.at[it, direction, slot, h])
                part = box[it, direction, slot, h]
                total = part if total is None else total + part
            return total

        for h in range(2):
            yo[it, h] = own_column(0, h) + last_sums(yb, "yr", h)
            for w in range(2):
                n = number(("owner", 2 * h + w))
                copy = pltpu.make_async_remote_copy(
                    src_ref=yo.at[it, h, w], dst_ref=fa.at[it, xh, column_k],
                    send_sem=send_sem.at[n], recv_sem=recv_sem.at[it, N_KEYS - 8 + column_k * 2 + xh],
                    device_id=stations[2 * h + w], device_id_type=MESH,
                )
                copy.start()
                sends.append(copy)
        for k in range(2):
            for h in range(2):
                pltpu.make_async_remote_copy(
                    src_ref=fa.at[it, h, k], dst_ref=fa.at[it, h, k],
                    send_sem=send_sem.at[0], recv_sem=recv_sem.at[it, N_KEYS - 8 + k * 2 + h],
                    device_id=core_peer, device_id_type=MESH,
                ).wait_recv()
        fm[it] = fa[it, 0] + fa[it, 1]
        push(("home",), fm.at[it], fr.at[it], served)
        for h in range(2):
            xs[it, h] = own_row(0, h) + last_sums(zb, "zr", h)
        push(("xr",), xs.at[it, 1 - xi], xr.at[it], x_peer)

        bytes_of_fifteen(gram_recv.at[it, 1])
        held = o_ref[...]
        below = jnp.dot(
            held.reshape(128, 128), gf[it].reshape(128, 128),
            precision=lax.Precision.HIGHEST, preferred_element_type=F32,
        ).reshape(2, 2, 32, 128)
        arrived(("xr",), xr.at[it])
        arrived(("home",), fr.at[it])
        product = xs[it, xi] + xr[it]
        for k in range(2):
            above = product[:, k] + fr[it, k]
            o_ref[:, k] = held[:, k] * (0.5 + 0.5 * above / below[:, k])

        for copy in sends:
            copy.wait_send()
        for phase in range(2):
            bytes_of_fifteen(gram_send.at[phase])
        assert len(keys) <= N_KEYS - 8
        return carry

    lax.fori_loop(0, ITERS, sweep, 0)


def shards(tiles, tile_blocks, tile_count, factor):
    vmem = pl.BlockSpec(memory_space=pltpu.VMEM)
    smem = pl.BlockSpec(memory_space=pltpu.SMEM)
    held = pl.pallas_call(
        kernel,
        out_shape=jax.ShapeDtypeStruct((2, 2, 32, 128), F32),
        in_specs=[smem, smem, pl.BlockSpec(memory_space=pl.ANY), vmem],
        out_specs=vmem,
        scratch_shapes=[
            pltpu.VMEM((2, 1024, 1024), BF16),
            pltpu.VMEM((2, 8, 2, 2, 2, 2, 32, 128), BF16),
            pltpu.VMEM((2, 8, 4, 2, 32, 128), BF16),
            pltpu.VMEM((2, 8, 2, 2, 2, 2, 32, 128), F32),
            pltpu.VMEM((2, 8, 2, 2, 2, 32, 128), F32),
            pltpu.VMEM((2, 2, 4, 2, 2, 2, 32, 128), F32),
            pltpu.VMEM((2, 8, 4, 2, 32, 128), F32),
            pltpu.VMEM((2, 2, 4, 2, 2, 2, 32, 128), F32),
            pltpu.VMEM((2, 2, 2, 2, 32, 128), F32),
            pltpu.VMEM((2, 2, 2, 32, 128), F32),
            pltpu.VMEM((2, 2, 2, 32, 128), F32),
            pltpu.VMEM((2, 16, 8, 128), F32),
            pltpu.VMEM((2, 15, 8, 128), F32),
            pltpu.VMEM((2, 16, 8, 128), F32),
            pltpu.VMEM((2, 128, 1024), F32),
            pltpu.VMEM((2, 1024, 128), BF16),
            pltpu.VMEM((2, 2, 2, 2, 32, 128), F32),
            pltpu.VMEM((2, 2, 2, 2, 32, 128), F32),
            pltpu.VMEM((2, 2, 2, 32, 128), F32),
            pltpu.SemaphoreType.DMA,
            pltpu.SemaphoreType.DMA((N_KEYS,)),
            pltpu.SemaphoreType.DMA((2, N_KEYS)),
            pltpu.SemaphoreType.DMA((2,)),
            pltpu.SemaphoreType.DMA((2, 2)),
        ],
        compiler_params=pltpu.CompilerParams(
            collective_id=0, has_side_effects=True, vmem_limit_bytes=50 * 1024 * 1024
        ),
    )(tile_blocks, tile_count, tiles, factor.reshape(2, 2, 32, 128))
    return held.reshape(factor.shape)


def solution(mesh):
    in_specs = (
        P(("row", "col"), None, None),
        P(("row", "col"), None),
        P(("row", "col")),
        P(None, None, "row", "col", None, None),
    )
    out_specs = P(None, None, "row", "col", None, None)
    return jax.shard_map(shards, mesh=mesh, in_specs=in_specs, out_specs=out_specs, check_vma=False)
```

time: 130 us -> 121 us (0.931); the launches traced: 128 us -> 121 us
  Pallas kernels: 125 us -> 118 us
    pallas_call x1, Pallas kernels: 125 us -> 118 us  [shards(): pl.pallas_call(kernel, out_shape=jax.ShapeDtypeStruct((2, 2, 32, 128), F3...]
where the time goes in v2:
time: 121 us
  Pallas kernels  118 us (98%)
  local copies, waits for them, and re-layouts  2.14 us (2%)
    pallas_call x1, Pallas kernels, shards(): pl.pallas_call(kernel, out_shape=jax.ShapeDtypeStruct((2, 2, 32, 128), F3...  118 us

profile of v2, /device:TPU:1, one launch (start us, length us, event | category | flops | bytes accessed | tf_op | source)
XLA Modules:
  0.0 120.6 jit_solution(9526006780582719850)
XLA Ops:
  0.7 0.0 copy-start
  0.7 0.8 copy-done
  1.5 0.0 copy-start.1
  1.5 0.7 copy-done.1
  2.2 117.8 %shard_map.46 = f32[2,2,32,128]{3,2,1,0:T(8,128)S(1)} custom-call(s32[2,2]{1,0:T(2,128)S(1)} %copy-done.1, s32[1]{0:T(128)S(6)} %copy.7.count, bf16[2,1024,1024]{2,1,0:T(8,128)(2,1)} %tiles_hbm.1, f32[2,2,32,128]{3,2,1,0:T(8,128)S(1)} %bitcast.5), custom_call_target="tpu_custom_call" | custom-call | tf_op jit(solution)/shard_map/pallas_call | solution.py:404
  120.0 0.6 copy.8
Async XLA Ops:
  0.7 0.8 copy-start
  1.5 0.7 copy-start.1

commit v3 on v2

--- a/solution.py
+++ b/solution.py
@@ -273,8 +273,6 @@
             for far, pos in zip(fars, places):
                 push(("cr", far), rs.at[it, pos, 1 - ka], cr.at[it, pos], core_peer)
 
-        row_chunks((4,))
-        row_chunks((3, 5))
         met = set()
 
         def own_row(far, h):
@@ -296,21 +294,21 @@
                 zb.at[it, direction, 0, h], z_next[direction],
             )
 
-        def pass_sums(slot):
+        def column_sums(slot):
             for direction, h in chains:
                 if slot < hops(direction, h) - 1:
-                    far = distance(direction, h, slot)
                     buf = yb.at[it, direction, slot, h]
                     arrived(("yr", direction, slot, h), buf)
-                    yb[it, direction, slot, h] += own_column(far, h)
+                    yb[it, direction, slot, h] += own_column(distance(direction, h, slot), h)
                     push(("yr", direction, slot + 1, h), buf, yb.at[it, direction, slot + 1, h], y_next[direction])
+
+        def row_sums(slot):
+            for direction, h in chains:
+                if slot < hops(direction, h) - 1:
                     buf = zb.at[it, direction, slot, h]
                     arrived(("zr", direction, slot, h), buf)
-                    zb[it, direction, slot, h] += own_row(far, h)
+                    zb[it, direction, slot, h] += own_row(distance(direction, h, slot), h)
                     push(("zr", direction, slot + 1, h), buf, zb.at[it, direction, slot + 1, h], z_next[direction])
-
-        for direction, h in chains:
-            first_sums(direction, h)
 
         def gram_scatter(d, carry):
             pltpu.make_async_remote_copy(
@@ -330,17 +328,6 @@
 
         def bytes_of_fifteen(sem):
             pltpu.make_async_copy(gr.at[it], gr.at[it], sem).wait()
-
-        lax.fori_loop(1, 16, gram_scatter, 0)
-        row_chunks((2, 6))
-        pass_sums(0)
-        row_chunks((1, 7))
-        pass_sums(1)
-        row_chunks((0,))
-        bytes_of_fifteen(gram_recv.at[it, 0])
-        gf[it, r] = gm[it, r] + jnp.sum(gr[it], axis=0)
-        lax.fori_loop(1, 16, gram_gather, 0)
-        pass_sums(2)
 
         def last_sums(box, name, h):
             total = None
@@ -351,6 +338,22 @@
                 total = part if total is None else total + part
             return total
 
+        row_chunks((4,))
+        row_chunks((3, 5))
+        column_sums(0)
+        for direction, h in chains:
+            first_sums(direction, h)
+        lax.fori_loop(1, 16, gram_scatter, 0)
+        row_chunks((2, 6))
+        column_sums(1)
+        row_sums(0)
+        row_chunks((1, 7))
+        column_sums(2)
+        row_sums(1)
+        row_chunks((0,))
+        bytes_of_fifteen(gram_recv.at[it, 0])
+        gf[it, r] = gm[it, r] + jnp.sum(gr[it], axis=0)
+        lax.fori_loop(1, 16, gram_gather, 0)
         for h in range(2):
             yo[it, h] = own_column(0, h) + last_sums(yb, "yr", h)
             for w in range(2):
@@ -362,6 +365,10 @@
                 )
                 copy.start()
                 sends.append(copy)
+        row_sums(2)
+        for h in range(2):
+            xs[it, h] = own_row(0, h) + last_sums(zb, "zr", h)
+        push(("xr",), xs.at[it, 1 - xi], xr.at[it], x_peer)
         for k in range(2):
             for h in range(2):
                 pltpu.make_async_remote_copy(
@@ -371,9 +378,6 @@
                 ).wait_recv()
         fm[it] = fa[it, 0] + fa[it, 1]
         push(("home",), fm.at[it], fr.at[it], served)
-        for h in range(2):
-            xs[it, h] = own_row(0, h) + last_sums(zb, "zr", h)
-        push(("xr",), xs.at[it, 1 - xi], xr.at[it], x_peer)
 
         bytes_of_fifteen(gram_recv.at[it, 1])
         held = o_ref[...]

time: 121 us -> 117 us (0.967)
  Pallas kernels: 118 us -> 114 us
    pallas_call x1, Pallas kernels: 118 us -> 114 us  [shards(): pl.pallas_call(kernel, out_shape=jax.ShapeDtypeStruct((2, 2, 32, 128), F3...]
where the time goes in v3:
time: 117 us
  Pallas kernels  114 us (97%)
  local copies, waits for them, and re-layouts  2.14 us (2%)
    pallas_call x1, Pallas kernels, shards(): pl.pallas_call(kernel, out_shape=jax.ShapeDtypeStruct((2, 2, 32, 128), F3...  114 us

profile of v3, /device:TPU:1, one launch (start us, length us, event | category | flops | bytes accessed | tf_op | source)
XLA Modules:
  0.0 116.9 jit_solution(16272816052497952567)
XLA Ops:
  0.7 0.0 copy-start
  0.7 0.8 copy-done
  1.5 0.0 copy-start.1
  1.5 0.7 copy-done.1
  2.2 114.1 %shard_map.46 = f32[2,2,32,128]{3,2,1,0:T(8,128)S(1)} custom-call(s32[2,2]{1,0:T(2,128)S(1)} %copy-done.1, s32[1]{0:T(128)S(6)} %copy.7.count, bf16[2,1024,1024]{2,1,0:T(8,128)(2,1)} %tiles_hbm.1, f32[2,2,32,128]{3,2,1,0:T(8,128)S(1)} %bitcast.5), custom_call_target="tpu_custom_call" | custom-call | tf_op jit(solution)/shard_map/pallas_call | solution.py:408
  116.3 0.6 copy.8
Async XLA Ops:
  0.7 0.8 copy-start
  1.5 0.7 copy-start.1

commit v4 on v3

--- a/solution.py
+++ b/solution.py
@@ -9,7 +9,7 @@
 MESH = pl.DeviceIdType.MESH
 F32 = jnp.float32
 BF16 = jnp.bfloat16
-N_KEYS = 112
+N_KEYS = 144
 
 
 def hops(direction, h):
@@ -114,9 +114,6 @@
         def row_piece(pos, h):
             return rp.at[it, pos, chain(h), ka]
 
-        def column_piece(pos, h):
-            return cp.at[it, pos, 2 * h:2 * h + 2]
-
         def pass_row(direction, step, h):
             pos = source_of(z, direction, step)
             piece = row_piece(pos, h)
@@ -126,11 +123,13 @@
                 push(("zg", direction, step + 1, h), piece, piece, z_next[direction])
 
         def pass_column(direction, step, h):
-            piece = column_piece(source_of(y, direction, step), h)
-            if step > 0:
-                arrived(("yg", direction, step, h), piece)
-            if step < hops(direction, h):
-                push(("yg", direction, step + 1, h), piece, piece, y_next[direction])
+            pos = source_of(y, direction, step)
+            for w in (2 * h, 2 * h + 1):
+                piece = cp.at[it, pos, w]
+                if step > 0:
+                    arrived(("yg", direction, step, w), piece)
+                if step < hops(direction, h):
+                    push(("yg", direction, step + 1, w), piece, piece, y_next[direction])
 
         def directions(step):
             return (0, 1) if 0 < step < 4 else (0,)
@@ -181,15 +180,6 @@
                         terms[s, :, columns] = term
                     else:
                         terms[s, :, columns] += term
-            total = None
-            for pos in places:
-                panel = rp[it, pos].reshape(512, 128)
-                part = jnp.dot(panel.T, panel, preferred_element_type=F32).reshape(16, 8, 128)
-                total = part if total is None else total + part
-            if step == 0:
-                gm[it] = total
-            else:
-                gm[it] += total
 
         push(("x",), mine, mine, x_peer)
         for direction in range(2):
@@ -242,10 +232,11 @@
 
         chains = ((0, 0), (1, 1), (0, 1), (1, 0))
         for direction, h in chains:
-            push(
-                ("yr", direction, 0, h), cs.at[it, (y + distance(direction, h, -1)) % 8, 2 * h:2 * h + 2],
-                yb.at[it, direction, 0, h], y_next[direction],
-            )
+            for w in (2 * h, 2 * h + 1):
+                push(
+                    ("yr", direction, 0, w), cs.at[it, (y + distance(direction, h, -1)) % 8, w],
+                    yb.at[it, direction, 0, w], y_next[direction],
+                )
         each(pass_column, 4)
 
         for s in range(2):
@@ -275,40 +266,49 @@
 
         met = set()
 
-        def own_row(far, h):
+        def own_row(far, h, p):
             pos = (z + far) % 8
             if far not in met:
                 met.add(far)
                 arrived(("cr", far), cr.at[it, pos])
-            return rs[it, pos, ka, h] + cr[it, pos, h]
-
-        def own_column(far, h):
-            return cs[it, (y + far) % 8, 2 * h:2 * h + 2]
-
-        def first_sums(direction, h):
+            return rs[it, pos, ka, h, p] + cr[it, pos, h, p]
+
+        def own_column(far, w):
+            return cs[it, (y + far) % 8, w]
+
+        def first_sums(direction, h, p):
             far = distance(direction, h, -1)
             pos = (z + far) % 8
-            rs[it, pos, ka, h] = own_row(far, h)
+            rs[it, pos, ka, h, p] = own_row(far, h, p)
             push(
-                ("zr", direction, 0, h), rs.at[it, pos, ka, h],
-                zb.at[it, direction, 0, h], z_next[direction],
+                ("zr", direction, 0, h, p), rs.at[it, pos, ka, h, p],
+                zb.at[it, direction, 0, h, p], z_next[direction],
             )
 
         def column_sums(slot):
-            for direction, h in chains:
-                if slot < hops(direction, h) - 1:
-                    buf = yb.at[it, direction, slot, h]
-                    arrived(("yr", direction, slot, h), buf)
-                    yb[it, direction, slot, h] += own_column(distance(direction, h, slot), h)
-                    push(("yr", direction, slot + 1, h), buf, yb.at[it, direction, slot + 1, h], y_next[direction])
+            for n in range(2):
+                for direction, h in chains:
+                    if slot < hops(direction, h) - 1:
+                        w = 2 * h + n
+                        buf = yb.at[it, direction, slot, w]
+                        arrived(("yr", direction, slot, w), buf)
+                        yb[it, direction, slot, w] += own_column(distance(direction, h, slot), w)
+                        push(
+                            ("yr", direction, slot + 1, w), buf,
+                            yb.at[it, direction, slot + 1, w], y_next[direction],
+                        )
 
         def row_sums(slot):
-            for direction, h in chains:
-                if slot < hops(direction, h) - 1:
-                    buf = zb.at[it, direction, slot, h]
-                    arrived(("zr", direction, slot, h), buf)
-                    zb[it, direction, slot, h] += own_row(distance(direction, h, slot), h)
-                    push(("zr", direction, slot + 1, h), buf, zb.at[it, direction, slot + 1, h], z_next[direction])
+            for p in range(2):
+                for direction, h in chains:
+                    if slot < hops(direction, h) - 1:
+                        buf = zb.at[it, direction, slot, h, p]
+                        arrived(("zr", direction, slot, h, p), buf)
+                        zb[it, direction, slot, h, p] += own_row(distance(direction, h, slot), h, p)
+                        push(
+                            ("zr", direction, slot + 1, h, p), buf,
+                            zb.at[it, direction, slot + 1, h, p], z_next[direction],
+                        )
 
         def gram_scatter(d, carry):
             pltpu.make_async_remote_copy(
@@ -329,20 +329,27 @@
         def bytes_of_fifteen(sem):
             pltpu.make_async_copy(gr.at[it], gr.at[it], sem).wait()
 
-        def last_sums(box, name, h):
+        def last_sums(box, name, h, *rest):
             total = None
             for direction in range(2):
                 slot = hops(direction, h) - 1
-                arrived((name, direction, slot, h), box.at[it, direction, slot, h])
-                part = box[it, direction, slot, h]
+                place = (it, direction, slot) + rest
+                arrived((name, direction, slot) + rest, box.at[place])
+                part = box[place]
                 total = part if total is None else total + part
             return total
 
         row_chunks((4,))
         row_chunks((3, 5))
         column_sums(0)
-        for direction, h in chains:
-            first_sums(direction, h)
+        for p in range(2):
+            for direction, h in chains:
+                first_sums(direction, h, p)
+        total = jnp.zeros((128, 128), F32)
+        for slot in range(4):
+            panel = rp[it, :, :, :, slot // 2, slot % 2].reshape(1024, 128)
+            total = total + jnp.dot(panel.T, panel, preferred_element_type=F32)
+        gm[it] = total.reshape(16, 8, 128)
         lax.fori_loop(1, 16, gram_scatter, 0)
         row_chunks((2, 6))
         column_sums(1)
@@ -354,20 +361,20 @@
         bytes_of_fifteen(gram_recv.at[it, 0])
         gf[it, r] = gm[it, r] + jnp.sum(gr[it], axis=0)
         lax.fori_loop(1, 16, gram_gather, 0)
-        for h in range(2):
-            yo[it, h] = own_column(0, h) + last_sums(yb, "yr", h)
-            for w in range(2):
-                n = number(("owner", 2 * h + w))
-                copy = pltpu.make_async_remote_copy(
-                    src_ref=yo.at[it, h, w], dst_ref=fa.at[it, xh, column_k],
-                    send_sem=send_sem.at[n], recv_sem=recv_sem.at[it, N_KEYS - 8 + column_k * 2 + xh],
-                    device_id=stations[2 * h + w], device_id_type=MESH,
-                )
-                copy.start()
-                sends.append(copy)
+        for w in (0, 2, 1, 3):
+            yo[it, w] = own_column(0, w) + last_sums(yb, "yr", w // 2, w)
+            n = number(("owner", w))
+            copy = pltpu.make_async_remote_copy(
+                src_ref=yo.at[it, w], dst_ref=fa.at[it, xh, column_k],
+                send_sem=send_sem.at[n], recv_sem=recv_sem.at[it, N_KEYS - 8 + column_k * 2 + xh],
+                device_id=stations[w], device_id_type=MESH,
+            )
+            copy.start()
+            sends.append(copy)
         row_sums(2)
-        for h in range(2):
-            xs[it, h] = own_row(0, h) + last_sums(zb, "zr", h)
+        for p in range(2):
+            for h in range(2):
+                xs[it, h, p] = own_row(0, h, p) + last_sums(zb, "zr", h, h, p)
         push(("xr",), xs.at[it, 1 - xi], xr.at[it], x_peer)
         for k in range(2):
             for h in range(2):
@@ -376,8 +383,12 @@
                     send_sem=send_sem.at[0], recv_sem=recv_sem.at[it, N_KEYS - 8 + k * 2 + h],
                     device_id=core_peer, device_id_type=MESH,
                 ).wait_recv()
-        fm[it] = fa[it, 0] + fa[it, 1]
-        push(("home",), fm.at[it], fr.at[it], served)
+            fm[it, k] = fa[it, 0, k] + fa[it, 1, k]
+            push(("home", k), fm.at[it, k], fr.at[it, k], served)
+        for copy in sends[:-2]:
+            copy.wait_send()
+        for phase in range(2):
+            bytes_of_fifteen(gram_send.at[phase])
 
         bytes_of_fifteen(gram_recv.at[it, 1])
         held = o_ref[...]
@@ -386,16 +397,15 @@
             precision=lax.Precision.HIGHEST, preferred_element_type=F32,
         ).reshape(2, 2, 32, 128)
         arrived(("xr",), xr.at[it])
-        arrived(("home",), fr.at[it])
+        for k in range(2):
+            arrived(("home", k), fr.at[it, k])
         product = xs[it, xi] + xr[it]
         for k in range(2):
             above = product[:, k] + fr[it, k]
             o_ref[:, k] = held[:, k] * (0.5 + 0.5 * above / below[:, k])
 
-        for copy in sends:
+        for copy in sends[-2:]:
             copy.wait_send()
-        for phase in range(2):
-            bytes_of_fifteen(gram_send.at[phase])
         assert len(keys) <= N_KEYS - 8
         return carry
 
@@ -418,7 +428,7 @@
             pltpu.VMEM((2, 8, 2, 2, 2, 32, 128), F32),
             pltpu.VMEM((2, 2, 4, 2, 2, 2, 32, 128), F32),
             pltpu.VMEM((2, 8, 4, 2, 32, 128), F32),
-            pltpu.VMEM((2, 2, 4, 2, 2, 2, 32, 128), F32),
+            pltpu.VMEM((2, 2, 4, 4, 2, 32, 128), F32),
             pltpu.VMEM((2, 2, 2, 2, 32, 128), F32),
             pltpu.VMEM((2, 2, 2, 32, 128), F32),
             pltpu.VMEM((2, 2, 2, 32, 128), F32),
@@ -427,7 +437,7 @@
             pltpu.VMEM((2, 16, 8, 128), F32),
             pltpu.VMEM((2, 128, 1024), F32),
             pltpu.VMEM((2, 1024, 128), BF16),
-            pltpu.VMEM((2, 2, 2, 2, 32, 128), F32),
+            pltpu.VMEM((2, 4, 2, 32, 128), F32),
             pltpu.VMEM((2, 2, 2, 2, 32, 128), F32),
             pltpu.VMEM((2, 2, 2, 32, 128), F32),
             pltpu.SemaphoreType.DMA,

time: 117 us -> 119 us (1.017)
  Pallas kernels: 114 us -> 116 us
    pallas_call x1, Pallas kernels: 114 us -> 116 us  [shards(): pl.pallas_call(kernel, out_shape=jax.ShapeDtypeStruct((2, 2, 32, 128), F3...]
where the time goes in v4:
time: 119 us
  Pallas kernels  116 us (97%)
  local copies, waits for them, and re-layouts  2.14 us (2%)
    pallas_call x1, Pallas kernels, shards(): pl.pallas_call(kernel, out_shape=jax.ShapeDtypeStruct((2, 2, 32, 128), F3...  116 us

profile of v4, /device:TPU:1, one launch (start us, length us, event | category | flops | bytes accessed | tf_op | source)
XLA Modules:
  0.0 118.6 jit_solution(13073249633553173190)
XLA Ops:
  0.7 0.0 copy-start
  0.7 0.8 copy-done
  1.5 0.0 copy-start.1
  1.5 0.7 copy-done.1
  2.2 115.8 %shard_map.46 = f32[2,2,32,128]{3,2,1,0:T(8,128)S(1)} custom-call(s32[2,2]{1,0:T(2,128)S(1)} %copy-done.1, s32[1]{0:T(128)S(6)} %copy.7.count, bf16[2,1024,1024]{2,1,0:T(8,128)(2,1)} %tiles_hbm.1, f32[2,2,32,128]{3,2,1,0:T(8,128)S(1)} %bitcast.5), custom_call_target="tpu_custom_call" | custom-call | tf_op jit(solution)/shard_map/pallas_call | solution.py:418
  118.0 0.6 copy.8
Async XLA Ops:
  0.7 0.8 copy-start
  1.5 0.7 copy-start.1

commit v5 on v3

--- a/solution.py
+++ b/solution.py
@@ -310,24 +310,42 @@
                     zb[it, direction, slot, h] += own_row(distance(direction, h, slot), h)
                     push(("zr", direction, slot + 1, h), buf, zb.at[it, direction, slot + 1, h], z_next[direction])
 
-        def gram_scatter(d, carry):
+        mine_to_sum = r % 4 == q
+
+        def gram_scatter(m, carry):
+            target = 4 * m + q
+
+            @pl.when(target != r)
+            def _():
+                pltpu.make_async_remote_copy(
+                    src_ref=gm.at[it, target], dst_ref=gr.at[it, (target + 16 - r) % 16 - 1],
+                    send_sem=gram_send.at[0], recv_sem=gram_recv.at[it, 0],
+                    device_id=(target, c), device_id_type=MESH,
+                ).start()
+
+            return carry
+
+        def gram_gather(d, carry):
+            piece = gf.at[it, r // 4, xi, ka]
             pltpu.make_async_remote_copy(
-                src_ref=gm.at[it, (r + d) % 16], dst_ref=gr.at[it, d - 1],
-                send_sem=gram_send.at[0], recv_sem=gram_recv.at[it, 0],
-                device_id=((r + d) % 16, c), device_id_type=MESH,
-            ).start()
-            return carry
-
-        def gram_gather(d, carry):
-            pltpu.make_async_remote_copy(
-                src_ref=gf.at[it, r], dst_ref=gf.at[it, r],
+                src_ref=piece, dst_ref=piece,
                 send_sem=gram_send.at[1], recv_sem=gram_recv.at[it, 1],
                 device_id=((r + d) % 16, c), device_id_type=MESH,
             ).start()
             return carry
 
-        def bytes_of_fifteen(sem):
-            pltpu.make_async_copy(gr.at[it], gr.at[it], sem).wait()
+        def bytes_of(pieces, sem):
+            box = gr.at[it, 0:pieces]
+            pltpu.make_async_copy(box, box, sem).wait()
+
+        def bytes_of_group(sem):
+            @pl.when(mine_to_sum)
+            def _():
+                bytes_of(3, sem)
+
+            @pl.when(jnp.logical_not(mine_to_sum))
+            def _():
+                bytes_of(4, sem)
 
         def last_sums(box, name, h):
             total = None
@@ -343,7 +361,7 @@
         column_sums(0)
         for direction, h in chains:
             first_sums(direction, h)
-        lax.fori_loop(1, 16, gram_scatter, 0)
+        lax.fori_loop(0, 4, gram_scatter, 0)
         row_chunks((2, 6))
         column_sums(1)
         row_sums(0)
@@ -351,9 +369,13 @@
         column_sums(2)
         row_sums(1)
         row_chunks((0,))
-        bytes_of_fifteen(gram_recv.at[it, 0])
-        gf[it, r] = gm[it, r] + jnp.sum(gr[it], axis=0)
-        lax.fori_loop(1, 16, gram_gather, 0)
+
+        @pl.when(mine_to_sum)
+        def _():
+            bytes_of(15, gram_recv.at[it, 0])
+            gf[it, r // 4, xi, ka] = gm[it, r] + jnp.sum(gr[it], axis=0)
+            lax.fori_loop(1, 16, gram_gather, 0)
+
         for h in range(2):
             yo[it, h] = own_column(0, h) + last_sums(yb, "yr", h)
             for w in range(2):
@@ -366,9 +388,13 @@
                 copy.start()
                 sends.append(copy)
         row_sums(2)
+        bytes_of_group(gram_recv.at[it, 1])
+        push(("gc",), gf.at[it, :, xi, ka], gf.at[it, :, xi, ka], core_peer)
         for h in range(2):
             xs[it, h] = own_row(0, h) + last_sums(zb, "zr", h)
         push(("xr",), xs.at[it, 1 - xi], xr.at[it], x_peer)
+        arrived(("gc",), gf.at[it, :, xi, 1 - ka])
+        push(("gx",), gf.at[it, :, xi], gf.at[it, :, xi], x_peer)
         for k in range(2):
             for h in range(2):
                 pltpu.make_async_remote_copy(
@@ -379,7 +405,7 @@
         fm[it] = fa[it, 0] + fa[it, 1]
         push(("home",), fm.at[it], fr.at[it], served)
 
-        bytes_of_fifteen(gram_recv.at[it, 1])
+        arrived(("gx",), gf.at[it, :, 1 - xi])
         held = o_ref[...]
         below = jnp.dot(
             held.reshape(128, 128), gf[it].reshape(128, 128),
@@ -394,8 +420,12 @@
 
         for copy in sends:
             copy.wait_send()
-        for phase in range(2):
-            bytes_of_fifteen(gram_send.at[phase])
+        bytes_of_group(gram_send.at[0])
+
+        @pl.when(mine_to_sum)
+        def _():
+            bytes_of(15, gram_send.at[1])
+
         assert len(keys) <= N_KEYS - 8
         return carry
 
@@ -424,7 +454,7 @@
             pltpu.VMEM((2, 2, 2, 32, 128), F32),
             pltpu.VMEM((2, 16, 8, 128), F32),
             pltpu.VMEM((2, 15, 8, 128), F32),
-            pltpu.VMEM((2, 16, 8, 128), F32),
+            pltpu.VMEM((2, 4, 2, 2, 8, 128), F32),
             pltpu.VMEM((2, 128, 1024), F32),
             pltpu.VMEM((2, 1024, 128), BF16),
             pltpu.VMEM((2, 2, 2, 2, 32, 128), F32),

time: 117 us -> 118 us (level)
  no operation moved by 1% of the time
where the time goes in v5:
time: 118 us; the launch traced here: 117 us
  Pallas kernels  114 us (97%)
  local copies, waits for them, and re-layouts  2.14 us (2%)
    pallas_call x1, Pallas kernels, shards(): pl.pallas_call(kernel, out_shape=jax.ShapeDtypeStruct((2, 2, 32, 128), F3...  114 us

profile of v5, /device:TPU:1, one launch (start us, length us, event | category | flops | bytes accessed | tf_op | source)
XLA Modules:
  0.0 116.8 jit_solution(14899534113069559104)
XLA Ops:
  0.7 0.0 copy-start
  0.7 0.8 copy-done
  1.5 0.0 copy-start.1
  1.5 0.7 copy-done.1
  2.2 114.0 %shard_map.46 = f32[2,2,32,128]{3,2,1,0:T(8,128)S(1)} custom-call(s32[2,2]{1,0:T(2,128)S(1)} %copy-done.1, s32[1]{0:T(128)S(6)} %copy.7.count, bf16[2,1024,1024]{2,1,0:T(8,128)(2,1)} %tiles_hbm.1, f32[2,2,32,128]{3,2,1,0:T(8,128)S(1)} %bitcast.5), custom_call_target="tpu_custom_call" | custom-call | tf_op jit(solution)/shard_map/pallas_call | solution.py:438
  116.2 0.6 copy.8
Async XLA Ops:
  0.7 0.8 copy-start
  1.5 0.7 copy-start.1
